TPU v7x, 32 devices: a whole 2x2x4 slice. The times are simulated.
32 devices in a mesh: row: 4 (over z), col: 8 (over y, x, core).
Axes of the slice: x: 2, y: 2, z: 4, core: 2. Of those that a mesh axis runs over, the one named last changes fastest.
Arguments:
- coefficients: float32 [4, 8, 2, 128, 1024], P('row', 'col'), may hold values from -1 to 1
- greens: float32 [8, 4, 1024], P('col'), may hold values from -1 to 1
- cosine_weights: float32 [2, 2], replicated, may hold values from 0.3 to 1.2
- block_atoms: int32 [4, 8, 2, 2], P('row', 'col'), may hold values from 0 to 7
- pair_blocks: int32 [4, 8, 8, 2], P('row', 'col'), may hold values from 0 to 1
- owner_row: int32 [4, 8, 8, 1], P('row', 'col'), may hold values from 0 to 3; in each aligned block of 8 rows (0 to 7, 8 to 15, ..., all dimensions but the last counted through in order) at most 4 rows name the same one
- target_sub: int32 [4, 8, 8], P('row', 'col'), may hold values from 0 to 15
Outputs:
- response: float32 [2, 2048, 4096], P(None, 'row', 'col')
Inputs may be any that keep to these rules, and one draw needn't show every extreme that they name: `owner_row`: among the 8 entries of one device (fixed first two indices) no row number occurs more than 4 times, and in every draw some device names one row exactly 4 times.
All inputs are finite; a program needn't handle non-finite values.
Results may differ from a plain program's by a relative error of at most 0.0029.
Values may be sent and summed in bfloat16 or wider, within the bound.
A program may use at most 64 MiB of HBM per device.

v0:
```python
import jax
import jax.numpy as jnp
from jax import lax
from jax.sharding import PartitionSpec as P

AUX_BLK = 128
BAS = 32
SUBS = 4
NCON = 8


HIGH = lax.Precision.HIGHEST


def swapped_2(block, axis, bit):
    count = lax.axis_size(axis)
    route = []
    for low in range(count):
        high = low | 1 << bit
        if high != low and high < count:
            route += [(low, high), (high, low)]
    return lax.ppermute(block, axis, route)


def accumulate(received, labels, mirrored):
    flat_count = labels.shape[0] * labels.shape[1]
    freq_count = received.shape[2]
    flat_labels = labels.reshape(flat_count)
    flat_data = received.reshape(flat_count, freq_count, AUX_BLK, AUX_BLK)
    sub_ids = jnp.arange(SUBS * SUBS, dtype=jnp.int32)
    if mirrored:
        swapped = flat_labels % SUBS * SUBS + flat_labels // SUBS
        flat_labels = jnp.where(flat_labels < 0, -1, swapped)
        selector = (flat_labels[:, None] == sub_ids[None, :]).astype(jnp.bfloat16)
        return jnp.einsum("ns,nfab->sfba", selector, flat_data, preferred_element_type=jnp.float32)
    selector = (flat_labels[:, None] == sub_ids[None, :]).astype(jnp.bfloat16)
    return jnp.einsum("ns,nfab->sfab", selector, flat_data, preferred_element_type=jnp.float32)


def assemble(summed):
    tiled = summed.reshape(SUBS, SUBS, 2, AUX_BLK, AUX_BLK)
    return tiled.transpose(2, 0, 3, 1, 4).reshape(2, SUBS * AUX_BLK, SUBS * AUX_BLK)


def collect_slots(received, labels):
    mirror_bit = lax.axis_size("col").bit_length() - 2
    partner_data, partner_labels = swapped_2((received, labels), "col", mirror_bit)
    return accumulate(received, labels, False) + accumulate(partner_data, partner_labels, True)


def local(coefficients, greens, cosine_weights, block_atoms, pair_blocks, owner_row, target_sub):
    blocks = coefficients[0, 0]
    count = blocks.shape[0]
    pair_width = blocks.shape[2]
    atom_pairs = block_atoms[0, 0]
    atom_total = greens.shape[0] * lax.axis_size("col")
    selector = (
        atom_pairs[:, :, None] == jnp.arange(atom_total, dtype=jnp.int32)[None, None, :]
    ).astype(jnp.float32)
    table = lax.all_gather(greens, "col", axis=0, tiled=True)
    chosen = jnp.einsum("bsa,ake->bske", selector, table, precision=HIGH)
    occupied = chosen[:, 0, 0:2].reshape(count, 2, BAS, BAS)
    virtual = chosen[:, 1, 2:4].reshape(count, 2, BAS, BAS)
    shaped = blocks.reshape(count, AUX_BLK, BAS, BAS)
    partway = jnp.einsum("bpmn,btns->btpms", shaped, virtual, precision=HIGH)
    contracted = jnp.einsum("btpms,btml->btpls", partway, occupied, precision=HIGH)
    combined = jnp.einsum("ft,btpls->bfpls", cosine_weights, contracted, precision=HIGH)
    combined = combined.reshape(count, 2, AUX_BLK, pair_width)
    every_pair = jnp.einsum("bfap,cqp->bcfaq", combined, blocks, precision=HIGH)
    every_pair = every_pair.reshape(count * count, 2, AUX_BLK, AUX_BLK).astype(jnp.bfloat16)
    block_pairs = pair_blocks[0, 0]
    pair_ids = block_pairs[:, 0] * count + block_pairs[:, 1]
    pair_onehot = (pair_ids[:, None] == jnp.arange(count * count, dtype=jnp.int32)[None, :]).astype(
        jnp.float32
    )
    row_count = lax.axis_size("row")
    capacity = max(2, 2 * NCON // row_count)
    owners = owner_row[0, 0, :, 0]
    targets = target_sub[0, 0]
    positions = jnp.arange(NCON, dtype=jnp.int32)
    earlier = (owners[:, None] == owners[None, :]) & (positions[None, :] < positions[:, None])
    slot_rank = jnp.sum(earlier.astype(jnp.int32), axis=1)
    placement = (owners[:, None, None] == jnp.arange(row_count, dtype=jnp.int32)[None, :, None]) & (
        slot_rank[:, None, None] == jnp.arange(capacity, dtype=jnp.int32)[None, None, :]
    )
    slot_pairs = jnp.einsum("krc,kp->rcp", placement.astype(jnp.float32), pair_onehot).astype(
        jnp.bfloat16
    )
    outgoing = jnp.einsum(
        "rcp,pfab->rcfab", slot_pairs, every_pair, preferred_element_type=jnp.float32
    ).astype(jnp.bfloat16)
    out_labels = jnp.sum(placement.astype(jnp.int32) * (targets + 1)[:, None, None], axis=0) - 1
    received, in_labels = (
        lax.all_to_all(outgoing, "row", split_axis=0, concat_axis=0, tiled=True),
        lax.all_to_all(out_labels, "row", split_axis=0, concat_axis=0, tiled=True),
    )
    summed = collect_slots(received, in_labels)
    return assemble(summed)


def solution(mesh):
    in_specs = (
        P("row", "col", None, None, None),
        P("col", None, None),
        P(),
        P("row", "col", None, None),
        P("row", "col", None, None),
        P("row", "col", None, None),
        P("row", "col", None),
    )
    out_specs = P(None, "row", "col")
    return jax.shard_map(local, mesh=mesh, in_specs=in_specs, out_specs=out_specs, check_vma=False)
```

profile of v0, /device:TPU:0, one launch (start us, length us, event | category | flops | bytes accessed | tf_op | source)
XLA Modules:
  0.0 93.6 jit_solution(4366043887713400112)
XLA Ops:
  0.0 1.6 %copy.40 = f32[1,1,2,128,1024]{3,4,2,1,0:T(8,128)S(1)} copy(f32[1,1,2,128,1024]{4,3,2,1,0:T(8,128)} %param.7) | data formatting | bytes 2097152 | tf_op args[0]
  1.6 10.7 %all_gather.3 = f32[8,4,1024]{2,1,0:T(4,128)S(1)} all-gather(f32[1,4,1024]{2,1,0:T(4,128)S(1)} %copy-done.2), channel_id=1, replica_groups=mesh['row'=4,'col'=8] {'col'}, dimensions={0}, use_global_device_ids=true | all-gather | bytes 147456 | tf_op jit(solution)/shard_map/all_gather | solution.py:60
  12.3 0.3 fusion.21
  12.6 0.1 slice_reduce_fusion.1
  12.7 0.1 reshape_squeeze.10
  12.8 0.1 reshape_squeeze.9
  12.9 1.8 %convolution_bitcast_fusion = f32[2,2,128,32,32]{2,4,3,1,0:T(8,128)S(1)} fusion(f32[2,128,32,32,1]{1,3,2,4,0:T(8,128)S(1)} %bitcast.92, f32[2,2,32,32]{3,2,1,0:T(8,128)S(1)} %reshape_squeeze.10), kind=kOutput, calls=%fused_computation.8 | convolution fusion | flops 201326592 | bytes 3162112 | tf_op jit(solution)/shard_map/bpmn,btns->btpms/dot_general | solution.py:65
  14.7 3.0 %fusion.6 = f32[2,2,128,32,32]{2,3,4,1,0:T(8,128)S(1)} fusion(f32[2,2,128,32,32]{2,4,3,1,0:T(8,128)S(1)} %convolution_bitcast_fusion, f32[2,2,32,32]{3,2,1,0:T(8,128)S(1)} %reshape_squeeze.9), kind=kOutput, calls=%fused_computation.7 | convolution fusion | flops 201326592 | bytes 4210688 | tf_op jit(solution)/shard_map/btpms,btml->btpls/dot_general | solution.py:66
  17.8 0.0 copy-start.1
  17.8 8.0 %fusion.4 = f32[2,128,32,32,2]{1,4,3,2,0:T(2,128)S(1)} fusion(f32[2,2,128,32,32]{2,3,4,1,0:T(8,128)S(1)} %fusion.6, f32[2,2]{1,0:T(2,128)S(1)} %copy-done), kind=kOutput, calls=%fused_computation.5 | convolution fusion | flops 12582912 | bytes 4194320 | tf_op jit(solution)/shard_map/ft,btpls->bfpls/dot_general | solution.py:67
  25.8 0.0 copy-start.4
  25.8 0.0 copy-start.5
  25.9 3.5 %fusion.12 = bf16[2,2,2,128,128]{4,3,1,2,0:T(8,128)(2,1)S(1)} fusion(f32[2,2,128,1024,1]{2,1,3,0,4:T(2,128)S(1)} %bitcast.91, f32[1,1,2,128,1024]{4,3,2,1,0:T(8,128)S(1)} %copy-done.1), kind=kOutput, calls=%fused_computation.11 | convolution fusion | flops 1610743808 | bytes 3407872 | tf_op jit(solution)/shard_map/bfap,cqp->bcfaq/dot_general | solution.py:69
  29.4 0.2 convert_reduce_fusion
  29.6 0.6 convolution_convert_fusion
  30.2 30.9 %all_to_all.14 = bf16[4,4,2,128,128]{4,1,3,2,0:T(4,128)(2,1)S(1)} all-to-all(bf16[4,4,2,128,128]{4,1,3,2,0:T(4,128)(2,1)S(1)} %convolution_convert_fusion), channel_id=1, replica_groups=mesh['row'=4,'col'=8] {'row'}, dimensions={0} | all-to-all | bytes 2097152 | tf_op jit(solution)/shard_map/all_to_all | solution.py:94
  61.1 1.5 %collective-permute-start = (bf16[4,4,2,128,128]{4,1,3,2,0:T(4,128)(2,1)S(1)}, bf16[4,4,2,128,128]{4,1,3,2,0:T(4,128)(2,1)}, u32[]{:S(2)}, u32[]{:S(2)}) collective-permute-start(bf16[4,4,2,128,128]{4,1,3,2,0:T(4,128)(2,1)S(1)} %all_to_all.14), channel_id=1, source_target_pairs={{0,4},{4,0},{1,5},{5,1},{2,6},{6,2},{3,7},{7,3},{8,12},{12,8},{9,1... | collective-permute-start | bytes 3145736 | tf_op jit(solution)/shard_map/ppermute | solution.py:22
  62.6 0.2 fusion.28
  62.8 8.1 %all_to_all.15 = s32[4,1,4]{2,1,0:T(1,128)S(1)} all-to-all(s32[4,1,4]{2,1,0:T(1,128)S(1)} %bitcast.97), channel_id=1, replica_groups=mesh['row'=4,'col'=8] {'row'}, dimensions={0} | all-to-all | bytes 128 | tf_op jit(solution)/shard_map/all_to_all | solution.py:95
  70.9 0.5 collective-permute-start.1
  71.4 0.5 broadcast.144
  71.9 0.7 reduce.7
  72.6 0.1 eq.121
  72.7 12.9 %collective-permute-done.1 = s32[4,4]{1,0:T(4,128)S(1)} collective-permute-done((s32[4,4]{1,0:T(4,128)S(1)}, s32[4,4]{1,0:T(4,128)S(1)}, u32[]{:S(2)}, u32[]{:S(2)}) %collective-permute-start.1) | collective-permute-done | bytes 96 | tf_op jit(solution)/shard_map/ppermute | solution.py:22
  85.6 0.1 reshape.146
  85.7 0.2 copy.48
  85.9 0.7 fusion.17
  86.6 1.5 %copy.50 = bf16[4,4,2,128,128]{4,3,2,1,0:T(8,128)(2,1)S(1)} copy(bf16[4,4,2,128,128]{4,1,3,2,0:T(4,128)(2,1)} %collective-permute-done) | data formatting | bytes 2097152 | tf_op jit(solution)/shard_map/ppermute | solution.py:22
  88.1 1.7 %copy.51 = bf16[16,2,128,128]{2,0,3,1:T(8,128)(2,1)} copy(bf16[16,2,128,128]{3,2,1,0:T(8,128)(2,1)S(1)} %bitcast.94) | data formatting | bytes 2097152 | tf_op jit(solution)/shard_map/reshape | solution.py:29
  89.8 1.6 %bitcast_add_fusion = f32[16,2,128,128]{3,0,2,1:T(8,128)S(1)} fusion(f32[16,2,128,128]{3,0,2,1:T(8,128)S(1)} %fusion.17, bf16[16,2,128,128]{2,0,3,1:T(8,128)(2,1)} %copy.51, s32[16]{0:T(128)S(1)} %fusion.52), kind=kOutput, calls=%fused_computation | convolution fusion | flops 17301760 | bytes 5242944 | tf_op jit(solution)/shard_map/ns,nfab->sfba/dot_general | solution.py:35
  91.4 0.4 copy.52
  91.8 1.8 %reshape.148 = f32[2,512,512]{2,1,0:T(8,128)} reshape(f32[2,4,128,4,128]{4,3,2,1,0:T(4,128)S(1)} %copy.52) | data formatting | bytes 4194304 | tf_op jit(solution)/shard_map/reshape | solution.py:42
  (18 shorter events, 0.1 us)
Async XLA Ops:
  0.0 17.8 %copy-start = (f32[2,2]{1,0:T(2,128)S(1)}, f32[2,2]{1,0:T(2,128)}, u32[]{:S(2)}) copy-start(f32[2,2]{1,0:T(2,128)} %param.9) | copy-start | bytes 52
  0.0 1.6 %copy-start.2 = (f32[1,4,1024]{2,1,0:T(4,128)S(1)}, f32[1,4,1024]{2,1,0:T(4,128)}, u32[]{:S(2)}) copy-start(f32[1,4,1024]{2,1,0:T(4,128)} %param.8) | copy-start | bytes 49156
  0.0 12.3 %copy-start.3 = (s32[1,1,2,2]{3,2,1,0:T(2,128)S(1)}, s32[1,1,2,2]{3,2,1,0:T(2,128)}, u32[]{:S(2)}) copy-start(s32[1,1,2,2]{3,2,1,0:T(2,128)} %param.10) | copy-start | bytes 52
  17.8 8.1 %copy-start.1 = (f32[1,1,2,128,1024]{4,3,2,1,0:T(8,128)S(1)}, f32[1,1,2,128,1024]{4,3,2,1,0:T(8,128)}, u32[]{:S(2)}) copy-start(f32[1,1,2,128,1024]{4,3,2,1,0:T(8,128)} %param.7) | copy-start | bytes 3145732
  25.8 3.6 %copy-start.4 = (s32[1,1,8,1]{2,3,1,0:T(1,128)S(1)}, s32[1,1,8,1]{2,3,1,0:T(1,128)}, u32[]{:S(2)}) copy-start(s32[1,1,8,1]{2,3,1,0:T(1,128)} %param.12) | copy-start | bytes 100
  25.8 3.8 %copy-start.5 = (s32[1,1,8,2]{2,3,1,0:T(2,128)S(1)}, s32[1,1,8,2]{2,3,1,0:T(2,128)}, u32[]{:S(2)}) copy-start(s32[1,1,8,2]{2,3,1,0:T(2,128)} %param.11) | copy-start | bytes 196
  29.4 33.3 %copy-start.6 = (s32[1,1,8]{2,1,0:T(1,128)S(1)}, s32[1,1,8]{2,1,0:T(1,128)}, u32[]{:S(2)}) copy-start(s32[1,1,8]{2,1,0:T(1,128)} %param.13) | copy-start | bytes 100
  61.1 25.5 %collective-permute-start = (bf16[4,4,2,128,128]{4,1,3,2,0:T(4,128)(2,1)S(1)}, bf16[4,4,2,128,128]{4,1,3,2,0:T(4,128)(2,1)}, u32[]{:S(2)}, u32[]{:S(2)}) collective-permute-start(bf16[4,4,2,128,128]{4,1,3,2,0:T(4,128)(2,1)S(1)} %all_to_all.14), channel_id=1, source_target_pairs={{0,4},{4,0},{1,5},{5,1},{2,6},{6,2},{3,7},{7,3},{8,12},{12,8},{9,1... | collective-permute-start | bytes 3145736 | tf_op jit(solution)/shard_map/ppermute | solution.py:22
  70.9 14.7 %collective-permute-start.1 = (s32[4,4]{1,0:T(4,128)S(1)}, s32[4,4]{1,0:T(4,128)S(1)}, u32[]{:S(2)}, u32[]{:S(2)}) collective-permute-start(s32[4,4]{1,0:T(4,128)S(1)} %bitcast.96), channel_id=1, source_target_pairs={{0,4},{4,0},{1,5},{5,1},{2,6},{6,2},{3,7},{7,3},{8,12},{12,8},{9,1... | collective-permute-start | bytes 200 | tf_op jit(solution)/shard_map/ppermute | solution.py:22
where the time goes:
time: 93.9 us; the launch traced here: 93.6 us
  blocking collectives  49.7 us (53%)
  matrix products  19.6 us (21%)
  waiting for transfers between devices  12.9 us (14%)
  local copies, waits for them, and re-layouts  8.19 us (9%)
  starting transfers between devices  2.03 us (2%)
  other arithmetic  1.04 us (1%)
    all_to_all x1, blocking collectives, local(): lax.all_to_all(outgoing, 'row', split_axis=0, concat_axis=0, tiled=True)  30.9 us
    ppermute x2, waiting for transfers between devices, swapped_2(): return lax.ppermute(block, axis, route)  12.9 us
    all_gather x1, blocking collectives, local(): table = lax.all_gather(greens, 'col', axis=0, tiled=True)  10.7 us
    all_to_all x1, blocking collectives, local(): lax.all_to_all(out_labels, 'row', split_axis=0, concat_axis=0, tiled=True)  8.08 us
    dot_general x1, matrix products, local(): jnp.einsum('ft,btpls->bfpls', cosine_weights, contracted, precision=HIGH)  8.04 us
    dot_general x1, matrix products, local(): every_pair = jnp.einsum('bfap,cqp->bcfaq', combined, blocks, precision=HIGH)  3.49 us
    dot_general x1, matrix products, local(): jnp.einsum('btpms,btml->btpls', partway, occupied, precision=HIGH)  3.02 us
    ppermute x2, starting transfers between devices, swapped_2(): return lax.ppermute(block, axis, route)  2.03 us
  transfers between devices with their start and end apart: 2, of which 1 were waited for; matrix products, arithmetic and copies ran while one was open for 3% of the time, Pallas kernels for 0%

commit v1 on v0

v1 whole, which is shorter than its diff:
```python
import functools

import jax
import jax.numpy as jnp
from jax import lax
from jax.experimental import pallas as pl
from jax.experimental.pallas import tpu as pltpu
from jax.sharding import PartitionSpec as P

AUX_BLK = 128
BAS = 32
SUBS = 4
LABEL_ROWS = 16
BF = jnp.bfloat16
F32 = jnp.float32
MESH = pl.DeviceIdType.MESH


def split(x):
    high = x.astype(BF)
    return high, (x - high.astype(F32)).astype(BF)


def dot(a, b, dims=((1,), (0,))):
    return lax.dot_general(a, b, (dims, ((), ())), preferred_element_type=F32)


def dot3(a, b, dims=((1,), (0,))):
    return dot(a[0], b[0], dims) + (dot(a[0], b[1], dims) + dot(a[1], b[0], dims))


def onehot(shape, row_key, col_key):
    rows = lax.broadcasted_iota(jnp.int32, shape, 0)
    cols = lax.broadcasted_iota(jnp.int32, shape, 1)
    return row_key(rows) == col_key(cols)


def kernel(
    n_row, n_col, w_ref, atoms_ref, green_ref, label_ref, coef_ref, out_ref,
    table, gath, prods, send_g, recv_g, send_l, send_r, send_y, recv_z, recv_y,
):
    me_r = lax.axis_index("row")
    me_c = lax.axis_index("col")
    half = n_col // 2
    mirror = lax.rem(me_c + half, n_col)
    per = green_ref.shape[0]
    has_left = me_r > 0
    has_right = me_r < n_row - 1

    barrier = pltpu.get_barrier_semaphore()

    def greet(step, carry):
        peer = lax.rem(me_c + step, n_col)
        pl.semaphore_signal(barrier, inc=1, device_id=(me_r, peer), device_id_type=MESH)
        return carry

    lax.fori_loop(1, n_col, greet, 0)

    @pl.when(has_left)
    def _():
        pl.semaphore_signal(barrier, inc=1, device_id=(me_r - 1, me_c), device_id_type=MESH)

    @pl.when(has_right)
    def _():
        pl.semaphore_signal(barrier, inc=1, device_id=(me_r + 1, me_c), device_id_type=MESH)

    pl.semaphore_wait(
        barrier, n_col - 1 + has_left.astype(jnp.int32) + has_right.astype(jnp.int32)
    )

    def green_copy(slot, step, peer):
        return pltpu.make_async_remote_copy(
            src_ref=green_ref,
            dst_ref=table.at[slot],
            send_sem=send_g.at[step],
            recv_sem=recv_g.at[slot],
            device_id=(me_r, peer),
            device_id_type=MESH,
        )

    def send_green(step, carry):
        green_copy(me_c, step, lax.rem(me_c + step, n_col)).start()
        return carry

    lax.fori_loop(1, n_col, send_green, 0)

    def item(side, s, p):
        rows = 2 * AUX_BLK + (LABEL_ROWS if p == 0 else 0)
        return gath.at[side, s, p, pl.ds(0, rows)]

    def z_copy(s, p, to_right):
        sems = send_r if to_right else send_l
        return pltpu.make_async_remote_copy(
            src_ref=item(0, s, p),
            dst_ref=item(0, s, p),
            send_sem=sems.at[s, p],
            recv_sem=recv_z.at[s, p],
            device_id=(me_r + 1 if to_right else me_r - 1, me_c),
            device_id_type=MESH,
        )

    def y_copy(s, p):
        return pltpu.make_async_remote_copy(
            src_ref=item(0, s, p),
            dst_ref=item(1, s, p),
            send_sem=send_y.at[s, p],
            recv_sem=recv_y.at[s, p],
            device_id=(me_r, mirror),
            device_id_type=MESH,
        )

    out_ref[...] = jnp.zeros_like(out_ref)
    table[me_c] = green_ref[...]
    gath[0, me_r, 0, 2 * AUX_BLK :, :] = label_ref[...]
    coef = [split(coef_ref[q]) for q in range(2)]
    coef_all = tuple(jnp.concatenate([coef[q][h] for q in range(2)], 0) for h in range(2))
    wide = 8 * BAS
    rep_tile = onehot((wide, BAS), lambda i: i % BAS, lambda k: k).astype(BF)
    rep_each = onehot((wide, BAS), lambda i: i // 8, lambda k: k).astype(BF)
    lane_tile = jnp.concatenate(
        [onehot((4 * BAS, wide), lambda k: k, lambda j, t=t: (2 + t) * BAS + j % BAS) for t in range(2)], 1
    ).astype(F32).astype(BF)
    lane_each = jnp.concatenate(
        [onehot((4 * BAS, wide), lambda k: k, lambda j, t=t: t * BAS + j // 8) for t in range(2)], 1
    ).astype(F32).astype(BF)
    mask_tile = onehot((wide, 2 * wide), lambda i: i // BAS, lambda j: (j % wide) // BAS)
    mask_each = onehot((wide, 2 * wide), lambda i: i % 8, lambda j: j % 8)
    later = lax.broadcasted_iota(jnp.int32, (1, 2 * wide), 1) >= wide

    def wait_green(step, carry):
        peer = lax.rem(me_c + step, n_col)
        green_copy(peer, step, peer).wait_recv()
        return carry

    lax.fori_loop(1, n_col, wait_green, 0)

    for p in range(2):
        first = atoms_ref[p, 0]
        second = atoms_ref[p, 1]
        occ = split(table[first // per, first % per] if per > 1 else table[first, 0])
        vir = split(table[second // per, second % per] if per > 1 else table[second, 0])
        virt = []
        for part in vir:
            spread = dot(dot(rep_tile, part).astype(BF), lane_tile)
            spread = jnp.where(mask_tile, spread, 0.0)
            virt.append(jnp.concatenate([spread[:, :wide], spread[:, wide:]], 0).astype(BF))
        occupied = sum(dot(dot(rep_each, part).astype(BF), lane_each) for part in occ)
        occupied = jnp.where(mask_each, occupied, 0.0)
        left = split(
            jnp.concatenate(
                [occupied * jnp.where(later, w_ref[f, 1], w_ref[f, 0]) for f in range(2)], 0
            )
        )
        stacked = tuple(
            jnp.concatenate([part[:, m * wide : (m + 1) * wide] for m in range(4)], 0) for part in coef[p]
        )
        partway = dot3(virt, stacked, ((1,), (1,))).reshape(2, 8, 4, 8, 4 * AUX_BLK)
        lanes = []
        for s_hi in range(4):
            parts = [
                partway[:, :, s_hi, :, m * AUX_BLK : (m + 1) * AUX_BLK].reshape(2, 1, 8, 8, AUX_BLK)
                for m in range(4)
            ]
            lanes.append(jnp.concatenate(parts, 1).reshape(512, AUX_BLK))
        moved = split(jnp.concatenate(lanes, 1))
        combined = dot3(left, moved).reshape(2, BAS, 8, 4 * AUX_BLK)
        lanes = []
        for f in range(2):
            parts = [
                combined[f, :, :, s_hi * AUX_BLK : (s_hi + 1) * AUX_BLK].reshape(BAS, 1, 8, AUX_BLK)
                for s_hi in range(4)
            ]
            lanes.append(jnp.concatenate(parts, 1).reshape(BAS * BAS, AUX_BLK))
        right = split(jnp.concatenate(lanes, 1))
        gath[0, me_r, p, pl.ds(0, 2 * AUX_BLK), :] = dot3(coef_all, right).astype(BF)
        y_copy(me_r, p).start()

        @pl.when(has_right)
        def _(p=p):
            z_copy(me_r, p, True).start()

        @pl.when(has_left)
        def _(p=p):
            z_copy(me_r, p, False).start()

    def assemble(side, s):
        labels = gath[side, s, 0, 2 * AUX_BLK :, 0:AUX_BLK].astype(F32)
        code = jnp.where(labels[8:16] == me_r.astype(F32), labels[0:8], -1.0)
        for p in range(2):
            for q in range(2):
                for f in range(2):
                    block = gath[
                        side, s, p, q * AUX_BLK : (q + 1) * AUX_BLK, f * AUX_BLK : (f + 1) * AUX_BLK
                    ].astype(F32)
                    prods[f, 2 * p + q] = block.T if side == 0 else block

        def tile_row(i, carry):
            rows = pl.ds(pl.multiple_of(i * AUX_BLK, AUX_BLK), AUX_BLK)
            for j in range(SUBS):
                sub = i * SUBS + j if side == 0 else j * SUBS + i
                counts = [
                    jnp.sum(
                        jnp.where(code == (sub * 4 + k).astype(F32), 1.0, 0.0), axis=0, keepdims=True
                    )
                    for k in range(4)
                ]
                for f in range(2):
                    cols = slice(j * AUX_BLK, (j + 1) * AUX_BLK)
                    total = out_ref[f, rows, cols]
                    for k in range(4):
                        total += counts[k] * prods[f, k]
                    out_ref[f, rows, cols] = total
            return carry

        lax.fori_loop(0, SUBS, tile_row, 0)

    assemble(0, me_r)

    def pass_on(dist, carry):
        low = me_r - dist
        high = me_r + dist
        for p in range(2):

            @pl.when(low >= 0)
            def _(p=p):
                z_copy(low, p, True).wait_recv()
                y_copy(low, p).start()

                @pl.when(has_right)
                def _():
                    z_copy(low, p, True).start()

            @pl.when(high < n_row)
            def _(p=p):
                z_copy(high, p, False).wait_recv()
                y_copy(high, p).start()

                @pl.when(has_left)
                def _():
                    z_copy(high, p, False).start()

        @pl.when(low >= 0)
        def _():
            assemble(0, low)

        @pl.when(high < n_row)
        def _():
            assemble(0, high)

        return carry

    lax.fori_loop(1, n_row, pass_on, 0)

    def take_mirror(s):
        for p in range(2):
            y_copy(s, p).wait_recv()
        assemble(1, s)

    take_mirror(me_r)

    def mirrored(dist, carry):
        @pl.when(me_r - dist >= 0)
        def _():
            take_mirror(me_r - dist)

        @pl.when(me_r + dist < n_row)
        def _():
            take_mirror(me_r + dist)

        return carry

    lax.fori_loop(1, n_row, mirrored, 0)

    def drain_green(step, carry):
        green_copy(me_c, step, lax.rem(me_c + step, n_col)).wait_send()
        return carry

    lax.fori_loop(1, n_col, drain_green, 0)

    def drain(s, carry):
        for p in range(2):
            y_copy(s, p).wait_send()

            @pl.when(has_right & (s <= me_r))
            def _(p=p):
                z_copy(s, p, True).wait_send()

            @pl.when(has_left & (s >= me_r))
            def _(p=p):
                z_copy(s, p, False).wait_send()

        return carry

    lax.fori_loop(0, n_row, drain, 0)


def local(n_row, n_col, coefficients, greens, cosine_weights, block_atoms, pair_blocks, owner_row, target_sub):
    per = greens.shape[0]
    turned = greens.reshape(per, 4, BAS, BAS).transpose(0, 3, 1, 2).reshape(per, BAS, 4 * BAS)
    pairs = pair_blocks[0, 0]
    codes = target_sub[0, 0] * 4 + pairs[:, 0] * 2 + pairs[:, 1]
    labels = jnp.concatenate([codes, owner_row[0, 0, :, 0]]).astype(BF)
    labels = jnp.broadcast_to(labels[:, None], (LABEL_ROWS, 2 * AUX_BLK))
    vmem = pl.BlockSpec(memory_space=pltpu.VMEM)
    smem = pl.BlockSpec(memory_space=pltpu.SMEM)
    tile = SUBS * AUX_BLK
    dma = pltpu.SemaphoreType.DMA
    return pl.pallas_call(
        functools.partial(kernel, n_row, n_col),
        out_shape=jax.ShapeDtypeStruct((2, tile, tile), F32),
        in_specs=[smem, smem, vmem, vmem, vmem],
        out_specs=vmem,
        scratch_shapes=[
            pltpu.VMEM((n_col, per, BAS, 4 * BAS), F32),
            pltpu.VMEM((2, n_row, 2, 2 * AUX_BLK + LABEL_ROWS, 2 * AUX_BLK), BF),
            pltpu.VMEM((2, 4, AUX_BLK, AUX_BLK), F32),
            dma((n_col,)),
            dma((n_col,)),
            dma((n_row, 2)),
            dma((n_row, 2)),
            dma((n_row, 2)),
            dma((n_row, 2)),
            dma((n_row, 2)),
        ],
        compiler_params=pltpu.CompilerParams(
            collective_id=0, has_side_effects=True, vmem_limit_bytes=48 * 1024 * 1024
        ),
    )(cosine_weights, block_atoms[0, 0], turned, labels, coefficients[0, 0])


def solution(mesh):
    in_specs = (
        P("row", "col", None, None, None),
        P("col", None, None),
        P(),
        P("row", "col", None, None),
        P("row", "col", None, None),
        P("row", "col", None, None),
        P("row", "col", None),
    )
    return jax.shard_map(
        functools.partial(local, mesh.shape["row"], mesh.shape["col"]),
        mesh=mesh,
        in_specs=in_specs,
        out_specs=P(None, "row", "col"),
        check_vma=False,
    )
```

time: 93.9 us -> 44.5 us (0.47)
  blocking collectives: 49.7 us -> 0 us
  Pallas kernels: 0 us -> 37.8 us
  matrix products: 19.6 us -> 0 us
  waiting for transfers between devices: 12.9 us -> 0 us
  local copies, waits for them, and re-layouts: 8.19 us -> 4.96 us
  starting transfers between devices: 2.03 us -> 0 us
    all_to_all x2 -> x0, blocking collectives: 39 us -> none  [the longest x1 30.9 us: local(): lax.all_to_all(outgoing, 'row', split_axis=0, concat_axis=0, tiled=True)]
    pallas_call x0 -> x1, Pallas kernels: none -> 37.8 us  [local(): pl.pallas_call(functools.partial(kernel, n_row, n_col), out_shape=jax.Sha...]
    dot_general x8 -> x0, matrix products: 19.6 us -> none  [the longest x1 8.04 us: local(): jnp.einsum('ft,btpls->bfpls', cosine_weights, contracted, precision=HIGH)]
    ppermute x2 -> x0, waiting for transfers between devices: 12.9 us -> none  [swapped_2(): return lax.ppermute(block, axis, route)]
    all_gather x1 -> x0, blocking collectives: 10.7 us -> none  [local(): table = lax.all_gather(greens, 'col', axis=0, tiled=True)]
    reshape x3, local copies, waits for them, and re-layouts: 3.6 us -> 0.99 us  [local(): greens.reshape(per, 4, BAS, BAS).transpose(0, 3, 1, 2)]
    unnamed x15 -> x7, local copies, waits for them, and re-layouts: 1.63 us -> 3.9 us
    ppermute x2 -> x0, starting transfers between devices: 2.03 us -> none  [swapped_2(): return lax.ppermute(block, axis, route)]
  transfers between devices with their start and end apart: 2 -> 0, of which waited for: 1 -> 0; matrix products, arithmetic and copies ran while one was open for 3% -> 0% of each run, Pallas kernels for 0% -> 0%
where the time goes in v1:
time: 44.5 us; the launch traced here: 44.3 us
  Pallas kernels  37.8 us (85%)
  local copies, waits for them, and re-layouts  4.96 us (11%)
  other arithmetic  1.5 us (3%)
    pallas_call x1, Pallas kernels, local(): pl.pallas_call(functools.partial(kernel, n_row, n_col), out_shape=jax.Sha...  37.8 us
    unnamed x7, local copies, waits for them, and re-layouts  3.9 us
    concatenate x3, other arithmetic, local(): labels = jnp.concatenate([codes, owner_row[0, 0, :, 0]]).astype(BF)  1.5 us
    reshape x3, local copies, waits for them, and re-layouts, local(): greens.reshape(per, 4, BAS, BAS).transpose(0, 3, 1, 2)  0.99 us

profile of v1, /device:TPU:0, one launch (start us, length us, event | category | flops | bytes accessed | tf_op | source)
XLA Modules:
  0.0 44.3 jit_solution(12823756557848976857)
XLA Ops:
  0.0 0.8 %fusion.2 = bf16[8]{0:T(256)(128)(2,1)S(1)} fusion(s32[8,2]{0,1:T(2,128)} %bitcast.19, s32[1,1,8]{2,1,0:T(1,128)} %param.13), kind=kLoop, calls=%fused_computation.4 | loop fusion | flops 40 | bytes 112 | tf_op jit(solution)/shard_map/concatenate | solution.py:302
  0.8 0.7 %convert_bitcast_fusion = bf16[8]{0:T(256)(128)(2,1)S(1)} fusion(s32[1,1,8,1]{2,3,1,0:T(1,128)} %param.12), kind=kLoop, calls=%fused_computation.5 | loop fusion | flops 8 | bytes 48 | tf_op jit(solution)/shard_map/concatenate | solution.py:302
  1.4 0.1 pad_maximum_fusion
  1.5 0.1 broadcast_in_dim.2.label_ref
  1.6 0.8 %reshape.32 = f32[1,4,32,32]{3,2,1,0:T(8,128)S(1)} reshape(f32[1,4,1024]{2,1,0:T(4,128)} %param.8) | data formatting | bytes 32768 | tf_op jit(solution)/shard_map/reshape | solution.py:299
  2.4 0.1 copy.8
  2.5 0.1 reshape.33.green_ref
  2.6 0.0 copy-start
  2.6 1.2 %copy-done = f32[1,1,2,128,1024]{4,3,2,1,0:T(8,128)S(1)} copy-done((f32[1,1,2,128,1024]{4,3,2,1,0:T(8,128)S(1)}, f32[1,1,2,128,1024]{4,3,2,1,0:T(8,128)}, u32[]{:S(2)}) %copy-start) | copy-done | bytes 1048600
  3.8 0.0 copy-start.1
  3.8 0.7 %copy-done.1 = f32[2,2]{1,0:T(2,128)S(1)} copy-done((f32[2,2]{1,0:T(2,128)S(1)}, f32[2,2]{1,0:T(2,128)}, u32[]{:S(2)}) %copy-start.1) | copy-done | bytes 40
  4.5 0.0 copy-start.2
  4.5 0.7 %copy-done.2 = s32[1,1,2,2]{3,2,1,0:T(2,128)S(1)} copy-done((s32[1,1,2,2]{3,2,1,0:T(2,128)S(1)}, s32[1,1,2,2]{3,2,1,0:T(2,128)}, u32[]{:S(2)}) %copy-start.2) | copy-done | bytes 40
  5.2 37.8 %shard_map.73 = f32[2,512,512]{2,1,0:T(8,128)S(1)} custom-call(f32[2,2]{1,0:T(2,128)S(1)} %copy-done.1, s32[2,2]{1,0:T(2,128)S(1)} %bitcast.17, f32[1,32,128]{2,1,0:T(8,128)S(1)} %reshape.33.green_ref, bf16[16,256]{1,0:T(8,128)(2,1)S(1)} %broadcast_in_dim.2.label_ref, f32[2,128,1024]{2,1,0:T(8,128)S(1)} %bitcast.16), custom_call_target="tpu_custom_call" | custom-call | tf_op jit(solution)/shard_map/pallas_call | solution.py:308
  42.9 1.3 %copy.10 = f32[2,512,512]{2,1,0:T(8,128)} copy(f32[2,512,512]{2,1,0:T(8,128)S(1)} %shard_map.73) | data formatting | bytes 4194304
Async XLA Ops:
  2.6 1.2 %copy-start = (f32[1,1,2,128,1024]{4,3,2,1,0:T(8,128)S(1)}, f32[1,1,2,128,1024]{4,3,2,1,0:T(8,128)}, u32[]{:S(2)}) copy-start(f32[1,1,2,128,1024]{4,3,2,1,0:T(8,128)} %param.7) | copy-start | bytes 3145732
  3.8 0.7 %copy-start.1 = (f32[2,2]{1,0:T(2,128)S(1)}, f32[2,2]{1,0:T(2,128)}, u32[]{:S(2)}) copy-start(f32[2,2]{1,0:T(2,128)} %w_ref.1) | copy-start | bytes 52
  4.5 0.7 %copy-start.2 = (s32[1,1,2,2]{3,2,1,0:T(2,128)S(1)}, s32[1,1,2,2]{3,2,1,0:T(2,128)}, u32[]{:S(2)}) copy-start(s32[1,1,2,2]{3,2,1,0:T(2,128)} %param.10) | copy-start | bytes 52

commit v2 on v1

--- a/solution.py
+++ b/solution.py
@@ -36,8 +36,9 @@
 
 
 def kernel(
-    n_row, n_col, w_ref, atoms_ref, green_ref, label_ref, coef_ref, out_ref,
-    table, gath, prods, send_g, recv_g, send_l, send_r, send_y, recv_z, recv_y,
+    n_row, n_col, w_hbm, atoms_hbm, pairs_hbm, owners_hbm, targets_hbm, green_ref, coef_hbm, out_ref,
+    w_ref, atoms_ref, pairs_ref, owners_ref, targets_ref, coef_ref,
+    table, gath, prods, load, send_g, recv_g, send_l, send_r, send_y, recv_z, recv_y,
 ):
     me_r = lax.axis_index("row")
     me_c = lax.axis_index("col")
@@ -47,6 +48,14 @@
     has_left = me_r > 0
     has_right = me_r < n_row - 1
 
+    sources = (coef_hbm, green_ref, w_hbm, atoms_hbm, pairs_hbm, owners_hbm, targets_hbm)
+    places = (coef_ref, table.at[me_c], w_ref, atoms_ref, pairs_ref, owners_ref, targets_ref)
+    loads = [
+        pltpu.make_async_copy(source, place, load.at[number])
+        for number, (source, place) in enumerate(zip(sources, places))
+    ]
+    for copy in loads:
+        copy.start()
     barrier = pltpu.get_barrier_semaphore()
 
     def greet(step, carry):
@@ -110,22 +119,28 @@
         )
 
     out_ref[...] = jnp.zeros_like(out_ref)
-    table[me_c] = green_ref[...]
-    gath[0, me_r, 0, 2 * AUX_BLK :, :] = label_ref[...]
+    wide = 8 * BAS
+    flat = BAS * BAS
+    low_tile = onehot((flat, wide), lambda k: k // BAS, lambda j: j % BAS).astype(F32).astype(BF)
+    low_each = onehot((flat, wide), lambda k: k // BAS, lambda j: j // 8).astype(F32).astype(BF)
+    rep_each = onehot((wide, BAS), lambda i: i // 8, lambda k: k).astype(F32).astype(BF)
+    row_pick = onehot((BAS, flat), lambda i: i, lambda k: k % BAS)
+    mask_tile = onehot((wide, wide), lambda i: i // BAS, lambda j: j // BAS)
+    mask_each = onehot((wide, wide), lambda i: i % 8, lambda j: j % 8)
+    for copy in loads:
+        copy.wait()
+    diagonal = onehot((8, 8), lambda i: i, lambda j: j)
+    pairs = pairs_ref[...]
+    codes = targets_ref[...] * 4 + pairs[0:1] * 2 + pairs[1:2]
+    labels = [
+        jnp.broadcast_to(
+            jnp.sum(jnp.where(diagonal, row.astype(F32), 0.0), axis=1, keepdims=True), (8, 2 * AUX_BLK)
+        )
+        for row in (codes, owners_ref[...])
+    ]
+    gath[0, me_r, 0, 2 * AUX_BLK :, :] = jnp.concatenate(labels, 0).astype(BF)
     coef = [split(coef_ref[q]) for q in range(2)]
     coef_all = tuple(jnp.concatenate([coef[q][h] for q in range(2)], 0) for h in range(2))
-    wide = 8 * BAS
-    rep_tile = onehot((wide, BAS), lambda i: i % BAS, lambda k: k).astype(BF)
-    rep_each = onehot((wide, BAS), lambda i: i // 8, lambda k: k).astype(BF)
-    lane_tile = jnp.concatenate(
-        [onehot((4 * BAS, wide), lambda k: k, lambda j, t=t: (2 + t) * BAS + j % BAS) for t in range(2)], 1
-    ).astype(F32).astype(BF)
-    lane_each = jnp.concatenate(
-        [onehot((4 * BAS, wide), lambda k: k, lambda j, t=t: t * BAS + j // 8) for t in range(2)], 1
-    ).astype(F32).astype(BF)
-    mask_tile = onehot((wide, 2 * wide), lambda i: i // BAS, lambda j: (j % wide) // BAS)
-    mask_each = onehot((wide, 2 * wide), lambda i: i % 8, lambda j: j % 8)
-    later = lax.broadcasted_iota(jnp.int32, (1, 2 * wide), 1) >= wide
 
     def wait_green(step, carry):
         peer = lax.rem(me_c + step, n_col)
@@ -137,18 +152,36 @@
     for p in range(2):
         first = atoms_ref[p, 0]
         second = atoms_ref[p, 1]
-        occ = split(table[first // per, first % per] if per > 1 else table[first, 0])
-        vir = split(table[second // per, second % per] if per > 1 else table[second, 0])
+        own = table[first // per, first % per] if per > 1 else table[first, 0]
+        other = table[second // per, second % per] if per > 1 else table[second, 0]
+        occ = split(
+            jnp.concatenate([jnp.where(row_pick, own[t : t + 1], 0.0) for t in range(2)], 0)
+        )
+        vir = split(
+            jnp.concatenate([jnp.where(row_pick, other[2 + t : 3 + t], 0.0) for t in range(2)], 0)
+        )
         virt = []
         for part in vir:
-            spread = dot(dot(rep_tile, part).astype(BF), lane_tile)
-            spread = jnp.where(mask_tile, spread, 0.0)
-            virt.append(jnp.concatenate([spread[:, :wide], spread[:, wide:]], 0).astype(BF))
-        occupied = sum(dot(dot(rep_each, part).astype(BF), lane_each) for part in occ)
-        occupied = jnp.where(mask_each, occupied, 0.0)
+            spread = dot(part, low_tile)
+            blocks = [
+                jnp.where(mask_tile, jnp.concatenate([spread[t * BAS : (t + 1) * BAS]] * 8, 0), 0.0)
+                for t in range(2)
+            ]
+            virt.append(jnp.concatenate(blocks, 0).astype(BF))
+        spread = [dot(part, low_each).astype(BF) for part in occ]
+        occupied = [
+            jnp.where(
+                mask_each, sum(dot(rep_each, part[t * BAS : (t + 1) * BAS]) for part in spread), 0.0
+            )
+            for t in range(2)
+        ]
         left = split(
             jnp.concatenate(
-                [occupied * jnp.where(later, w_ref[f, 1], w_ref[f, 0]) for f in range(2)], 0
+                [
+                    jnp.concatenate([occupied[t] * w_ref[f, t] for t in range(2)], 1)
+                    for f in range(2)
+                ],
+                0,
             )
         )
         stacked = tuple(
@@ -296,24 +329,26 @@
 
 def local(n_row, n_col, coefficients, greens, cosine_weights, block_atoms, pair_blocks, owner_row, target_sub):
     per = greens.shape[0]
-    turned = greens.reshape(per, 4, BAS, BAS).transpose(0, 3, 1, 2).reshape(per, BAS, 4 * BAS)
-    pairs = pair_blocks[0, 0]
-    codes = target_sub[0, 0] * 4 + pairs[:, 0] * 2 + pairs[:, 1]
-    labels = jnp.concatenate([codes, owner_row[0, 0, :, 0]]).astype(BF)
-    labels = jnp.broadcast_to(labels[:, None], (LABEL_ROWS, 2 * AUX_BLK))
+    hbm = pl.BlockSpec(memory_space=pltpu.HBM)
     vmem = pl.BlockSpec(memory_space=pltpu.VMEM)
-    smem = pl.BlockSpec(memory_space=pltpu.SMEM)
     tile = SUBS * AUX_BLK
     dma = pltpu.SemaphoreType.DMA
     return pl.pallas_call(
         functools.partial(kernel, n_row, n_col),
         out_shape=jax.ShapeDtypeStruct((2, tile, tile), F32),
-        in_specs=[smem, smem, vmem, vmem, vmem],
+        in_specs=[hbm] * 7,
         out_specs=vmem,
         scratch_shapes=[
-            pltpu.VMEM((n_col, per, BAS, 4 * BAS), F32),
+            pltpu.SMEM((2, 2), F32),
+            pltpu.SMEM((2, 2), jnp.int32),
+            pltpu.VMEM((2, 8), jnp.int32),
+            pltpu.VMEM((1, 8), jnp.int32),
+            pltpu.VMEM((1, 8), jnp.int32),
+            pltpu.VMEM((2, AUX_BLK, BAS * BAS), F32),
+            pltpu.VMEM((n_col, per, 4, BAS * BAS), F32),
             pltpu.VMEM((2, n_row, 2, 2 * AUX_BLK + LABEL_ROWS, 2 * AUX_BLK), BF),
             pltpu.VMEM((2, 4, AUX_BLK, AUX_BLK), F32),
+            dma((7,)),
             dma((n_col,)),
             dma((n_col,)),
             dma((n_row, 2)),
@@ -323,9 +358,17 @@
             dma((n_row, 2)),
         ],
         compiler_params=pltpu.CompilerParams(
-            collective_id=0, has_side_effects=True, vmem_limit_bytes=48 * 1024 * 1024
+            collective_id=0, has_side_effects=True, vmem_limit_bytes=60 * 1024 * 1024
         ),
-    )(cosine_weights, block_atoms[0, 0], turned, labels, coefficients[0, 0])
+    )(
+        cosine_weights,
+        block_atoms[0, 0],
+        pair_blocks[0, 0].T,
+        owner_row[0, 0].T,
+        target_sub[0],
+        greens,
+        coefficients[0, 0],
+    )
 
 
 def solution(mesh):

time: 44.5 us -> 42.1 us (0.946)
  local copies, waits for them, and re-layouts: 4.96 us -> 3.08 us
  other arithmetic: 1.5 us -> 0 us
  Pallas kernels: 37.8 us -> 38.8 us
    concatenate x3 -> x0, other arithmetic: 1.5 us -> none  [local(): labels = jnp.concatenate([codes, owner_row[0, 0, :, 0]]).astype(BF)]
    pallas_call x1, Pallas kernels: 37.8 us -> 38.8 us  [local(): pl.pallas_call(functools.partial(kernel, n_row, n_col), out_shape=jax.Sha...]
    reshape x3 -> x0, local copies, waits for them, and re-layouts: 0.99 us -> none  [local(): greens.reshape(per, 4, BAS, BAS).transpose(0, 3, 1, 2)]
    unnamed x7 -> x1, local copies, waits for them, and re-layouts: 3.9 us -> 3.08 us
where the time goes in v2:
time: 42.1 us; the launch traced here: 41.9 us
  Pallas kernels  38.8 us (92%)
  local copies, waits for them, and re-layouts  3.08 us (7%)
    pallas_call x1, Pallas kernels, local(): pl.pallas_call(functools.partial(kernel, n_row, n_col), out_shape=jax.Sha...  38.8 us
    unnamed x1, local copies, waits for them, and re-layouts  3.08 us

profile of v2, /device:TPU:0, one launch (start us, length us, event | category | flops | bytes accessed | tf_op | source)
XLA Modules:
  0.0 41.9 jit_solution(3559166889270026872)
XLA Ops:
  0.0 38.8 %shard_map.73 = f32[2,512,512]{2,1,0:T(8,128)} custom-call(f32[2,2]{1,0:T(2,128)} %w_hbm.1, s32[2,2]{1,0:T(2,128)} %bitcast.8, s32[2,8]{1,0:T(2,128)} %bitcast.9, s32[1,8]{1,0:T(1,128)} %bitcast.10, s32[1,8]{1,0:T(1,128)} %bitcast.11, f32[1,4,1024]{2,1,0:T(4,128)} %green_ref.1, f32[2,128,1024]{2,1,0:T(8,128)} %bitcast.7), custom_call_target="tpu_custom_call" | custom-call | tf_op jit(solution)/shard_map/pallas_call | solution.py:336
  38.9 3.1 %copy.9 = f32[2,512,512]{2,1,0:T(8,128)} copy(f32[2,512,512]{2,1,0:T(8,128)} %shard_map.73) | data formatting | bytes 4194304

commit v3 on v2

--- a/solution.py
+++ b/solution.py
@@ -38,13 +38,14 @@
 def kernel(
     n_row, n_col, w_hbm, atoms_hbm, pairs_hbm, owners_hbm, targets_hbm, green_ref, coef_hbm, out_ref,
     w_ref, atoms_ref, pairs_ref, owners_ref, targets_ref, coef_ref,
-    table, gath, prods, load, send_g, recv_g, send_l, send_r, send_y, recv_z, recv_y,
+    table, gath, prods, load, send_g, recv_g, send_l, send_r, send_y, send_m, recv_z, recv_y,
 ):
     me_r = lax.axis_index("row")
     me_c = lax.axis_index("col")
     half = n_col // 2
     mirror = lax.rem(me_c + half, n_col)
     per = green_ref.shape[0]
+    buddy = me_r + 1 - 2 * lax.rem(me_r, 2)
     has_left = me_r > 0
     has_right = me_r < n_row - 1
 
@@ -73,6 +74,7 @@
     def _():
         pl.semaphore_signal(barrier, inc=1, device_id=(me_r + 1, me_c), device_id_type=MESH)
 
+    out_ref[...] = jnp.zeros_like(out_ref)
     pl.semaphore_wait(
         barrier, n_col - 1 + has_left.astype(jnp.int32) + has_right.astype(jnp.int32)
     )
@@ -118,7 +120,6 @@
             device_id_type=MESH,
         )
 
-    out_ref[...] = jnp.zeros_like(out_ref)
     wide = 8 * BAS
     flat = BAS * BAS
     low_tile = onehot((flat, wide), lambda k: k // BAS, lambda j: j % BAS).astype(F32).astype(BF)
@@ -249,6 +250,25 @@
 
     assemble(0, me_r)
 
+    def handed_copy():
+        return pltpu.make_async_remote_copy(
+            src_ref=item(1, me_r, 1),
+            dst_ref=item(1, me_r, 1),
+            send_sem=send_m.at[0],
+            recv_sem=recv_y.at[me_r, 1],
+            device_id=(buddy, me_c),
+            device_id_type=MESH,
+        )
+
+    def pass_mirror(s, p):
+        if p == 0:
+            y_copy(s, p).start()
+        else:
+
+            @pl.when(s != buddy)
+            def _():
+                y_copy(s, p).start()
+
     def pass_on(dist, carry):
         low = me_r - dist
         high = me_r + dist
@@ -257,7 +277,7 @@
             @pl.when(low >= 0)
             def _(p=p):
                 z_copy(low, p, True).wait_recv()
-                y_copy(low, p).start()
+                pass_mirror(low, p)
 
                 @pl.when(has_right)
                 def _():
@@ -266,7 +286,7 @@
             @pl.when(high < n_row)
             def _(p=p):
                 z_copy(high, p, False).wait_recv()
-                y_copy(high, p).start()
+                pass_mirror(high, p)
 
                 @pl.when(has_left)
                 def _():
@@ -283,26 +303,34 @@
         return carry
 
     lax.fori_loop(1, n_row, pass_on, 0)
+
+    y_copy(me_r, 1).wait_recv()
+    handed_copy().start()
+    y_copy(me_r, 0).wait_recv()
+    assemble(1, me_r)
 
     def take_mirror(s):
         for p in range(2):
             y_copy(s, p).wait_recv()
         assemble(1, s)
 
-    take_mirror(me_r)
-
     def mirrored(dist, carry):
-        @pl.when(me_r - dist >= 0)
+        low = me_r - dist
+        high = me_r + dist
+
+        @pl.when((low >= 0) & (low != buddy))
         def _():
-            take_mirror(me_r - dist)
-
-        @pl.when(me_r + dist < n_row)
+            take_mirror(low)
+
+        @pl.when((high < n_row) & (high != buddy))
         def _():
-            take_mirror(me_r + dist)
+            take_mirror(high)
 
         return carry
 
     lax.fori_loop(1, n_row, mirrored, 0)
+    take_mirror(buddy)
+    handed_copy().wait_send()
 
     def drain_green(step, carry):
         green_copy(me_c, step, lax.rem(me_c + step, n_col)).wait_send()
@@ -312,7 +340,10 @@
 
     def drain(s, carry):
         for p in range(2):
-            y_copy(s, p).wait_send()
+
+            @pl.when((s != buddy) if p == 1 else (s >= 0))
+            def _(p=p):
+                y_copy(s, p).wait_send()
 
             @pl.when(has_right & (s <= me_r))
             def _(p=p):
@@ -335,7 +366,7 @@
     dma = pltpu.SemaphoreType.DMA
     return pl.pallas_call(
         functools.partial(kernel, n_row, n_col),
-        out_shape=jax.ShapeDtypeStruct((2, tile, tile), F32),
+        out_shape=pltpu.VMEM((2, tile, tile), F32),
         in_specs=[hbm] * 7,
         out_specs=vmem,
         scratch_shapes=[
@@ -354,6 +385,7 @@
             dma((n_row, 2)),
             dma((n_row, 2)),
             dma((n_row, 2)),
+            dma((1,)),
             dma((n_row, 2)),
             dma((n_row, 2)),
         ],

time: 42.1 us -> 39.5 us (0.938)
  local copies, waits for them, and re-layouts: 3.08 us -> 1.32 us
  Pallas kernels: 38.8 us -> 38 us
    unnamed x1, local copies, waits for them, and re-layouts: 3.08 us -> 1.32 us
    pallas_call x1, Pallas kernels: 38.8 us -> 38 us  [local(): pl.pallas_call(functools.partial(kernel, n_row, n_col), out_shape=pltpu.V...]
where the time goes in v3:
time: 39.5 us; the launch traced here: 39.4 us
  Pallas kernels  38 us (96%)
  local copies, waits for them, and re-layouts  1.32 us (3%)
    pallas_call x1, Pallas kernels, local(): pl.pallas_call(functools.partial(kernel, n_row, n_col), out_shape=pltpu.V...  38 us
    unnamed x1, local copies, waits for them, and re-layouts  1.32 us

profile of v3, /device:TPU:0, one launch (start us, length us, event | category | flops | bytes accessed | tf_op | source)
XLA Modules:
  0.0 39.4 jit_solution(18165855560121456069)
XLA Ops:
  0.0 38.0 %shard_map.73 = f32[2,512,512]{2,1,0:T(8,128)S(1)} custom-call(f32[2,2]{1,0:T(2,128)} %w_hbm.1, s32[2,2]{1,0:T(2,128)} %bitcast.8, s32[2,8]{1,0:T(2,128)} %bitcast.9, s32[1,8]{1,0:T(1,128)} %bitcast.10, s32[1,8]{1,0:T(1,128)} %bitcast.11, f32[1,4,1024]{2,1,0:T(4,128)} %green_ref.1, f32[2,128,1024]{2,1,0:T(8,128)} %bitcast.7), custom_call_target="tpu_custom_call" | custom-call | tf_op jit(solution)/shard_map/pallas_call | solution.py:367
  38.1 1.3 %copy.9 = f32[2,512,512]{2,1,0:T(8,128)} copy(f32[2,512,512]{2,1,0:T(8,128)S(1)} %shard_map.73) | data formatting | bytes 4194304

commit v4 on v3

--- a/solution.py
+++ b/solution.py
@@ -38,7 +38,7 @@
 def kernel(
     n_row, n_col, w_hbm, atoms_hbm, pairs_hbm, owners_hbm, targets_hbm, green_ref, coef_hbm, out_ref,
     w_ref, atoms_ref, pairs_ref, owners_ref, targets_ref, coef_ref,
-    table, gath, prods, load, send_g, recv_g, send_l, send_r, send_y, send_m, recv_z, recv_y,
+    table, gath, prods, load, send_g, recv_g, send_z, send_y, send_m, recv_z, recv_y,
 ):
     me_r = lax.axis_index("row")
     me_c = lax.axis_index("col")
@@ -46,8 +46,6 @@
     mirror = lax.rem(me_c + half, n_col)
     per = green_ref.shape[0]
     buddy = me_r + 1 - 2 * lax.rem(me_r, 2)
-    has_left = me_r > 0
-    has_right = me_r < n_row - 1
 
     sources = (coef_hbm, green_ref, w_hbm, atoms_hbm, pairs_hbm, owners_hbm, targets_hbm)
     places = (coef_ref, table.at[me_c], w_ref, atoms_ref, pairs_ref, owners_ref, targets_ref)
@@ -66,18 +64,14 @@
 
     lax.fori_loop(1, n_col, greet, 0)
 
-    @pl.when(has_left)
-    def _():
-        pl.semaphore_signal(barrier, inc=1, device_id=(me_r - 1, me_c), device_id_type=MESH)
-
-    @pl.when(has_right)
-    def _():
-        pl.semaphore_signal(barrier, inc=1, device_id=(me_r + 1, me_c), device_id_type=MESH)
-
+    def greet_row(step, carry):
+        peer = lax.rem(me_r + step, n_row)
+        pl.semaphore_signal(barrier, inc=1, device_id=(peer, me_c), device_id_type=MESH)
+        return carry
+
+    lax.fori_loop(1, n_row, greet_row, 0)
     out_ref[...] = jnp.zeros_like(out_ref)
-    pl.semaphore_wait(
-        barrier, n_col - 1 + has_left.astype(jnp.int32) + has_right.astype(jnp.int32)
-    )
+    pl.semaphore_wait(barrier, n_col + n_row - 2)
 
     def green_copy(slot, step, peer):
         return pltpu.make_async_remote_copy(
@@ -99,14 +93,13 @@
         rows = 2 * AUX_BLK + (LABEL_ROWS if p == 0 else 0)
         return gath.at[side, s, p, pl.ds(0, rows)]
 
-    def z_copy(s, p, to_right):
-        sems = send_r if to_right else send_l
+    def z_copy(s, p, peer):
         return pltpu.make_async_remote_copy(
             src_ref=item(0, s, p),
             dst_ref=item(0, s, p),
-            send_sem=sems.at[s, p],
+            send_sem=send_z.at[peer, p],
             recv_sem=recv_z.at[s, p],
-            device_id=(me_r + 1 if to_right else me_r - 1, me_c),
+            device_id=(peer, me_c),
             device_id_type=MESH,
         )
 
@@ -209,13 +202,18 @@
         gath[0, me_r, p, pl.ds(0, 2 * AUX_BLK), :] = dot3(coef_all, right).astype(BF)
         y_copy(me_r, p).start()
 
-        @pl.when(has_right)
-        def _(p=p):
-            z_copy(me_r, p, True).start()
-
-        @pl.when(has_left)
-        def _(p=p):
-            z_copy(me_r, p, False).start()
+        def send_row(dist, carry, p=p):
+            @pl.when(me_r - dist >= 0)
+            def _():
+                z_copy(me_r, p, me_r - dist).start()
+
+            @pl.when(me_r + dist < n_row)
+            def _():
+                z_copy(me_r, p, me_r + dist).start()
+
+            return carry
+
+        lax.fori_loop(1, n_row, send_row, 0)
 
     def assemble(side, s):
         labels = gath[side, s, 0, 2 * AUX_BLK :, 0:AUX_BLK].astype(F32)
@@ -276,21 +274,13 @@
 
             @pl.when(low >= 0)
             def _(p=p):
-                z_copy(low, p, True).wait_recv()
+                z_copy(low, p, low).wait_recv()
                 pass_mirror(low, p)
-
-                @pl.when(has_right)
-                def _():
-                    z_copy(low, p, True).start()
 
             @pl.when(high < n_row)
             def _(p=p):
-                z_copy(high, p, False).wait_recv()
+                z_copy(high, p, high).wait_recv()
                 pass_mirror(high, p)
-
-                @pl.when(has_left)
-                def _():
-                    z_copy(high, p, False).start()
 
         @pl.when(low >= 0)
         def _():
@@ -345,13 +335,9 @@
             def _(p=p):
                 y_copy(s, p).wait_send()
 
-            @pl.when(has_right & (s <= me_r))
+            @pl.when(s != me_r)
             def _(p=p):
-                z_copy(s, p, True).wait_send()
-
-            @pl.when(has_left & (s >= me_r))
-            def _(p=p):
-                z_copy(s, p, False).wait_send()
+                z_copy(me_r, p, s).wait_send()
 
         return carry
 
@@ -384,7 +370,6 @@
             dma((n_col,)),
             dma((n_row, 2)),
             dma((n_row, 2)),
-            dma((n_row, 2)),
             dma((1,)),
             dma((n_row, 2)),
             dma((n_row, 2)),

time: 39.5 us -> 51.1 us (1.29)
  Pallas kernels: 38 us -> 49.7 us
    pallas_call x1, Pallas kernels: 38 us -> 49.7 us  [local(): pl.pallas_call(functools.partial(kernel, n_row, n_col), out_shape=pltpu.V...]
where the time goes in v4:
time: 51.1 us; the launch traced here: 51 us
  Pallas kernels  49.7 us (97%)
  local copies, waits for them, and re-layouts  1.32 us (3%)
    pallas_call x1, Pallas kernels, local(): pl.pallas_call(functools.partial(kernel, n_row, n_col), out_shape=pltpu.V...  49.7 us
    unnamed x1, local copies, waits for them, and re-layouts  1.32 us

profile of v4, /device:TPU:0, one launch (start us, length us, event | category | flops | bytes accessed | tf_op | source)
XLA Modules:
  0.0 51.0 jit_solution(3124991254035053070)
XLA Ops:
  0.0 49.7 %shard_map.73 = f32[2,512,512]{2,1,0:T(8,128)S(1)} custom-call(f32[2,2]{1,0:T(2,128)} %w_hbm.1, s32[2,2]{1,0:T(2,128)} %bitcast.8, s32[2,8]{1,0:T(2,128)} %bitcast.9, s32[1,8]{1,0:T(1,128)} %bitcast.10, s32[1,8]{1,0:T(1,128)} %bitcast.11, f32[1,4,1024]{2,1,0:T(4,128)} %green_ref.1, f32[2,128,1024]{2,1,0:T(8,128)} %bitcast.7), custom_call_target="tpu_custom_call" | custom-call | tf_op jit(solution)/shard_map/pallas_call | solution.py:353
  49.7 1.3 %copy.9 = f32[2,512,512]{2,1,0:T(8,128)} copy(f32[2,512,512]{2,1,0:T(8,128)S(1)} %shard_map.73) | data formatting | bytes 4194304

commit v5 on v3

--- a/solution.py
+++ b/solution.py
@@ -207,8 +207,6 @@
             lanes.append(jnp.concatenate(parts, 1).reshape(BAS * BAS, AUX_BLK))
         right = split(jnp.concatenate(lanes, 1))
         gath[0, me_r, p, pl.ds(0, 2 * AUX_BLK), :] = dot3(coef_all, right).astype(BF)
-        y_copy(me_r, p).start()
-
         @pl.when(has_right)
         def _(p=p):
             z_copy(me_r, p, True).start()
@@ -216,6 +214,8 @@
         @pl.when(has_left)
         def _(p=p):
             z_copy(me_r, p, False).start()
+
+        y_copy(me_r, p).start()
 
     def assemble(side, s):
         labels = gath[side, s, 0, 2 * AUX_BLK :, 0:AUX_BLK].astype(F32)
@@ -248,8 +248,6 @@
 
         lax.fori_loop(0, SUBS, tile_row, 0)
 
-    assemble(0, me_r)
-
     def handed_copy():
         return pltpu.make_async_remote_copy(
             src_ref=item(1, me_r, 1),
@@ -277,28 +275,22 @@
             @pl.when(low >= 0)
             def _(p=p):
                 z_copy(low, p, True).wait_recv()
-                pass_mirror(low, p)
 
                 @pl.when(has_right)
                 def _():
                     z_copy(low, p, True).start()
 
+                pass_mirror(low, p)
+
             @pl.when(high < n_row)
             def _(p=p):
                 z_copy(high, p, False).wait_recv()
-                pass_mirror(high, p)
 
                 @pl.when(has_left)
                 def _():
                     z_copy(high, p, False).start()
 
-        @pl.when(low >= 0)
-        def _():
-            assemble(0, low)
-
-        @pl.when(high < n_row)
-        def _():
-            assemble(0, high)
+                pass_mirror(high, p)
 
         return carry
 
@@ -306,6 +298,12 @@
 
     y_copy(me_r, 1).wait_recv()
     handed_copy().start()
+
+    def take_own(s, carry):
+        assemble(0, s)
+        return carry
+
+    lax.fori_loop(0, n_row, take_own, 0)
     y_copy(me_r, 0).wait_recv()
     assemble(1, me_r)
 

time: 39.5 us -> 40.7 us (1.030)
  Pallas kernels: 38 us -> 39.2 us
    pallas_call x1, Pallas kernels: 38 us -> 39.2 us  [local(): pl.pallas_call(functools.partial(kernel, n_row, n_col), out_shape=pltpu.V...]
where the time goes in v5:
time: 40.7 us; the launch traced here: 40.5 us
  Pallas kernels  39.2 us (96%)
  local copies, waits for them, and re-layouts  1.32 us (3%)
    pallas_call x1, Pallas kernels, local(): pl.pallas_call(functools.partial(kernel, n_row, n_col), out_shape=pltpu.V...  39.2 us
    unnamed x1, local copies, waits for them, and re-layouts  1.32 us

profile of v5, /device:TPU:0, one launch (start us, length us, event | category | flops | bytes accessed | tf_op | source)
XLA Modules:
  0.0 40.5 jit_solution(18005947187849497691)
XLA Ops:
  0.0 39.2 %shard_map.73 = f32[2,512,512]{2,1,0:T(8,128)S(1)} custom-call(f32[2,2]{1,0:T(2,128)} %w_hbm.1, s32[2,2]{1,0:T(2,128)} %bitcast.8, s32[2,8]{1,0:T(2,128)} %bitcast.9, s32[1,8]{1,0:T(1,128)} %bitcast.10, s32[1,8]{1,0:T(1,128)} %bitcast.11, f32[1,4,1024]{2,1,0:T(4,128)} %green_ref.1, f32[2,128,1024]{2,1,0:T(8,128)} %bitcast.7), custom_call_target="tpu_custom_call" | custom-call | tf_op jit(solution)/shard_map/pallas_call | solution.py:365
  39.2 1.3 %copy.9 = f32[2,512,512]{2,1,0:T(8,128)} copy(f32[2,512,512]{2,1,0:T(8,128)S(1)} %shard_map.73) | data formatting | bytes 4194304

commit v6 on v3

--- a/solution.py
+++ b/solution.py
@@ -207,8 +207,6 @@
             lanes.append(jnp.concatenate(parts, 1).reshape(BAS * BAS, AUX_BLK))
         right = split(jnp.concatenate(lanes, 1))
         gath[0, me_r, p, pl.ds(0, 2 * AUX_BLK), :] = dot3(coef_all, right).astype(BF)
-        y_copy(me_r, p).start()
-
         @pl.when(has_right)
         def _(p=p):
             z_copy(me_r, p, True).start()
@@ -216,6 +214,8 @@
         @pl.when(has_left)
         def _(p=p):
             z_copy(me_r, p, False).start()
+
+        y_copy(me_r, p).start()
 
     def assemble(side, s):
         labels = gath[side, s, 0, 2 * AUX_BLK :, 0:AUX_BLK].astype(F32)

time: 39.5 us -> 39.5 us (level)
  no operation moved by 1% of the time
where the time goes in v6:
time: 39.5 us; the launch traced here: 39.4 us
  Pallas kernels  38 us (96%)
  local copies, waits for them, and re-layouts  1.32 us (3%)
    pallas_call x1, Pallas kernels, local(): pl.pallas_call(functools.partial(kernel, n_row, n_col), out_shape=pltpu.V...  38 us
    unnamed x1, local copies, waits for them, and re-layouts  1.32 us

profile of v6, /device:TPU:0, one launch (start us, length us, event | category | flops | bytes accessed | tf_op | source)
XLA Modules:
  0.0 39.4 jit_solution(10990384207530409616)
XLA Ops:
  0.0 38.0 %shard_map.73 = f32[2,512,512]{2,1,0:T(8,128)S(1)} custom-call(f32[2,2]{1,0:T(2,128)} %w_hbm.1, s32[2,2]{1,0:T(2,128)} %bitcast.8, s32[2,8]{1,0:T(2,128)} %bitcast.9, s32[1,8]{1,0:T(1,128)} %bitcast.10, s32[1,8]{1,0:T(1,128)} %bitcast.11, f32[1,4,1024]{2,1,0:T(4,128)} %green_ref.1, f32[2,128,1024]{2,1,0:T(8,128)} %bitcast.7), custom_call_target="tpu_custom_call" | custom-call | tf_op jit(solution)/shard_map/pallas_call | solution.py:367
  38.1 1.3 %copy.9 = f32[2,512,512]{2,1,0:T(8,128)} copy(f32[2,512,512]{2,1,0:T(8,128)S(1)} %shard_map.73) | data formatting | bytes 4194304
